TPU v7x, 32 devices: a whole 2x2x4 slice. The times are simulated.
32 devices in a mesh: py: 8 (over z, x), pz: 4 (over y, core).
Axes of the slice: x: 2, y: 2, z: 4, core: 2. Of those that a mesh axis runs over, the one named last changes fastest.
Arguments:
- velocity: float32 [3, 288, 160, 2048], P(None, 'pz', 'py'), may hold values from -40 to 40
Outputs:
- filtered_velocity: float32 [3, 32, 16, 256], P(None, None, 'pz', 'py')
- stresses: float32 [6, 32, 16, 256], P(None, None, 'pz', 'py')
All inputs are finite; a program needn't handle non-finite values.
Results may differ from a plain program's by a relative error of at most 0.00007.
Values sent between devices are 32-bit elements; how exact they have to be, the bound alone decides.
A program may use at most 192 MiB of HBM per device.

v0:
```python
import jax
import jax.numpy as jnp
from jax import lax
from jax.sharding import PartitionSpec as P

spread_cells = 8.0
stress_pairs = ((0, 0), (0, 1), (0, 2), (1, 1), (1, 2), (2, 2))
highest = lax.Precision.HIGHEST


def gauss_norm():
    tap_range = jnp.arange(-16, 17).astype(jnp.float32)
    return jnp.sum(jnp.exp(-tap_range * tap_range / (2.0 * spread_cells * spread_cells)))


def taps_matrix(n_outputs):
    n_inputs = 8 * n_outputs + 32
    offsets = (
        jnp.arange(n_inputs).astype(jnp.float32)[:, None]
        - 8.0 * jnp.arange(n_outputs).astype(jnp.float32)[None, :]
        - 16.0
    )
    weights = jnp.exp(-offsets * offsets / (2.0 * spread_cells * spread_cells)) / gauss_norm()
    return jnp.where(jnp.abs(offsets) <= 16.0, weights, 0.0)


def circulant_taps(n_cells):
    n_outputs = n_cells // 8
    cell_idx = jnp.arange(n_cells)[:, None]
    out_idx = jnp.arange(n_outputs)[None, :]
    wrapped = jnp.remainder(cell_idx - 8 * out_idx + n_cells // 2, n_cells) - n_cells // 2
    offsets = wrapped.astype(jnp.float32)
    weights = jnp.exp(-offsets * offsets / (2.0 * spread_cells * spread_cells)) / gauss_norm()
    return jnp.where(jnp.abs(offsets) <= 16.0, weights, 0.0)


def filter_first(fields):
    n_fields, plane_rows, line_rows, n_cells = fields.shape
    result = jnp.einsum("fzyn,nk->kyfz", fields, circulant_taps(n_cells), precision=highest)
    return result.reshape(n_cells // 8, line_rows, n_fields * plane_rows)


def filter_second(moved):
    y_total = moved.shape[1]
    return jnp.einsum("kym,yj->kjm", moved, taps_matrix((y_total - 32) // 8), precision=highest)


def split_fields(both, n_fields_a, plane_rows):
    grouped = both.reshape(both.shape[0], both.shape[1], 9, plane_rows)
    first_part = grouped[:, :, 0:n_fields_a].reshape(both.shape[0], both.shape[1], -1)
    second_part = grouped[:, :, n_fields_a:9].reshape(both.shape[0], both.shape[1], -1)
    return (first_part, second_part)


def filter_third(moved, n_fields, n_sources, plane_rows):
    z_total = n_sources * plane_rows
    grouped = moved.reshape(moved.shape[0], moved.shape[1], n_sources, n_fields, plane_rows)
    table = taps_matrix((z_total - 32) // 8).reshape(n_sources, plane_rows, -1)
    return jnp.einsum("kjsfz,szi->fijk", grouped, table, precision=highest)


def on_device(velocity):
    plane_rows = velocity.shape[1]
    products = jnp.stack(
        [velocity[first_comp] * velocity[second_comp] for first_comp, second_comp in stress_pairs]
    )
    vel_first = filter_first(velocity)
    prod_first = filter_first(products)
    merged = jnp.concatenate([vel_first, prod_first], axis=2)
    moved = lax.all_to_all(merged, "py", split_axis=0, concat_axis=1, tiled=True)
    both_second = filter_second(moved)
    vel_second, prod_second = split_fields(both_second, 3, plane_rows)
    n_sources = lax.axis_size("pz")
    vel_planes, prod_planes = (
        lax.all_to_all(vel_second, "pz", split_axis=1, concat_axis=2, tiled=True),
        lax.all_to_all(prod_second, "pz", split_axis=1, concat_axis=2, tiled=True),
    )
    filtered_velocity = filter_third(vel_planes, 3, n_sources, plane_rows)
    filtered_products = filter_third(prod_planes, 6, n_sources, plane_rows)
    stresses = jnp.stack(
        [
            filtered_products[pair_index]
            - filtered_velocity[first_comp] * filtered_velocity[second_comp]
            for pair_index, (first_comp, second_comp) in enumerate(stress_pairs)
        ]
    )
    return (filtered_velocity, stresses)


def solution(mesh):
    placed = (P(None, "pz", "py", None),)
    return jax.shard_map(
        on_device,
        mesh=mesh,
        in_specs=placed,
        out_specs=(P(None, None, "pz", "py"), P(None, None, "pz", "py")),
        check_vma=False,
    )
```

profile of v0, /device:TPU:0, one launch (start us, length us, event | category | flops | bytes accessed | tf_op | source)
XLA Modules:
  0.0 704.0 jit_solution(7904877954452540442)
XLA Ops:
  0.6 0.6 fusion.85
  1.2 11.3 %multiply_dynamic-update-slice_fusion.5 = f32[6,72,20,2048]{3,1,2,0:T(8,128)} fusion(f32[3,72,20,2048]{3,1,2,0:T(8,128)} %param.1), kind=kLoop, calls=%fused_computation.8 | loop fusion | flops 2949119 | bytes 23592960
  12.5 13.6 %multiply_dynamic-update-slice_fusion.4 = f32[6,72,20,2048]{3,1,2,0:T(8,128)} fusion(f32[6,72,20,2048]{3,1,2,0:T(8,128)} %multiply_dynamic-update-slice_fusion.5, f32[3,72,20,2048]{3,1,2,0:T(8,128)} %param.1), kind=kLoop, calls=%fused_computation.7 | loop fusion | flops 2949120 | bytes 35389440
  26.1 13.6 %multiply_dynamic-update-slice_fusion.3 = f32[6,72,20,2048]{3,1,2,0:T(8,128)} fusion(f32[6,72,20,2048]{3,1,2,0:T(8,128)} %multiply_dynamic-update-slice_fusion.4, f32[3,72,20,2048]{3,1,2,0:T(8,128)} %param.1), kind=kLoop, calls=%fused_computation.6 | loop fusion | flops 2949120 | bytes 35389440
  39.8 11.2 %multiply_dynamic-update-slice_fusion.2 = f32[6,72,20,2048]{3,1,2,0:T(8,128)} fusion(f32[6,72,20,2048]{3,1,2,0:T(8,128)} %multiply_dynamic-update-slice_fusion.3, f32[3,72,20,2048]{3,1,2,0:T(8,128)} %param.1), kind=kLoop, calls=%fused_computation.5 | loop fusion | flops 2949120 | bytes 23592960
  50.9 13.6 %multiply_dynamic-update-slice_fusion.1 = f32[6,72,20,2048]{3,1,2,0:T(8,128)} fusion(f32[6,72,20,2048]{3,1,2,0:T(8,128)} %multiply_dynamic-update-slice_fusion.2, f32[3,72,20,2048]{3,1,2,0:T(8,128)} %param.1), kind=kLoop, calls=%fused_computation.4 | loop fusion | flops 2949120 | bytes 35389440
  64.5 11.1 %multiply_dynamic-update-slice_fusion = f32[6,72,20,2048]{3,1,2,0:T(8,128)} fusion(f32[6,72,20,2048]{3,1,2,0:T(8,128)} %multiply_dynamic-update-slice_fusion.1, f32[3,72,20,2048]{3,1,2,0:T(8,128)} %param.1), kind=kLoop, calls=%fused_computation.3 | loop fusion | flops 2949120 | bytes 23592960 | tf_op jit(solution)/shard_map/stack | solution.py:64
  75.6 37.3 %convolution_bitcast_fusion.1 = f32[256,20,3,72]{0,3,1,2:T(8,128)S(1)} fusion(f32[3,72,20,2048]{3,1,2,0:T(8,128)} %param.1, f32[]{:T(128)} %fusion.85, s32[256]{0:T(256)S(1)} %iota_multiply_fusion), kind=kOutput, calls=%fused_computation.14 | convolution fusion | flops 27190624256 | bytes 39814148 | tf_op jit(solution)/shard_map/fzyn,nk->kyfz/dot_general | solution.py:39
  112.9 67.4 %convolution_bitcast_fusion = f32[256,20,6,72]{0,3,1,2:T(8,128)S(1)} fusion(f32[6,72,20,2048]{3,1,2,0:T(8,128)} %multiply_dynamic-update-slice_fusion, f32[]{:T(128)} %fusion.85, s32[256]{0:T(256)S(1)} %iota_multiply_fusion), kind=kOutput, calls=%fused_computation.9 | convolution fusion | flops 54369714176 | bytes 79627264 | tf_op jit(solution)/shard_map/fzyn,nk->kyfz/dot_general | solution.py:39
  180.4 4.3 copy.17
  184.7 2.4 copy.16
  187.1 10.5 %pad_maximum_fusion = f32[256,20,648]{0,2,1:T(8,128)} fusion(f32[256,20,432]{0,2,1:T(8,128)} %bitcast.60, f32[256,20,216]{0,2,1:T(8,128)} %bitcast.61), kind=kLoop, calls=%fused_computation.2 | loop fusion | flops 3317760 | bytes 26542080 | tf_op jit(solution)/shard_map/concatenate | solution.py:69
  197.6 18.0 %copy.18 = f32[256,20,648]{2,1,0:T(8,128)} copy(f32[256,20,648]{0,2,1:T(8,128)} %pad_maximum_fusion) | data formatting | bytes 26542080 | tf_op jit(solution)/shard_map/concatenate | solution.py:69
  215.7 7.3 %all-to-all-start = ((f32[256,20,648]{2,1,0:T(8,128)}), f32[256,20,648]{2,1,0:T(8,128)}, u32[]{:S(2)}, u32[]{:S(2)}) async-start(f32[256,20,648]{2,1,0:T(8,128)} %copy.18), calls=%async_computation | async-start | bytes 37748736 | tf_op jit(solution)/shard_map/all_to_all | solution.py:70
  222.9 408.5 %all-to-all-done = f32[256,20,648]{2,1,0:T(8,128)} async-done(((f32[256,20,648]{2,1,0:T(8,128)}), f32[256,20,648]{2,1,0:T(8,128)}, u32[]{:S(2)}, u32[]{:S(2)}) %all-to-all-start) | async-done | bytes 13271072 | tf_op jit(solution)/shard_map/all_to_all | solution.py:70
  631.5 11.1 %copy.20 = f32[32,8,20,648]{3,0,2,1:T(8,128)S(1)} copy(f32[32,8,20,648]{3,2,0,1:T(8,128)} %bitcast.12) | data formatting | bytes 26542080 | tf_op jit(solution)/shard_map/all_to_all | solution.py:70
  642.5 17.1 %fusion.14 = f32[32,16,648]{2,1,0:T(8,128)S(1)} fusion(f32[32,160,648]{2,0,1:T(8,128)S(1)} %bitcast.59, f32[]{:T(128)} %fusion.85, f32[16]{0:T(128)S(1)} %convert_multiply_fusion, f32[160]{0:T(256)S(1)} %iota_convert_fusion), kind=kOutput, calls=%fused_computation.26 | convolution fusion | flops 637032960 | bytes 14598852 | tf_op jit(solution)/shard_map/kym,yj->kjm/dot_general | solution.py:45
  659.6 3.4 reshape.79
  663.0 1.8 slice.74
  664.7 0.4 reshape.80
  665.2 1.1 copy.22
  666.3 4.1 all-to-all-start.1
  670.4 2.5 slice.75
  672.9 0.4 reshape.82
  673.3 1.6 copy.25
  674.9 4.4 all-to-all-done.1
  679.3 3.7 all-to-all-start.2
  683.0 1.1 copy.48
  684.1 0.4 reshape.81
  684.6 2.6 convolution_bitcast_fusion.2
  687.2 0.8 copy.28
  688.0 9.4 %all-to-all-done.2 = f32[32,16,432]{2,0,1:T(8,128)S(1)} async-done(((f32[32,16,432]{2,0,1:T(8,128)}), f32[32,16,432]{2,0,1:T(8,128)S(1)}, u32[]{:S(2)}, u32[]{:S(2)}) %all-to-all-start.2) | async-done | bytes 884768 | tf_op jit(solution)/shard_map/all_to_all | solution.py:76
  697.4 0.1 copy.47
  697.5 0.7 reshape.83
  698.2 4.5 fusion.17
  702.9 1.0 copy.29
  (11 shorter events, 0.1 us)
Async XLA Ops:
  215.7 415.8 %all-to-all-start = ((f32[256,20,648]{2,1,0:T(8,128)}), f32[256,20,648]{2,1,0:T(8,128)}, u32[]{:S(2)}, u32[]{:S(2)}) async-start(f32[256,20,648]{2,1,0:T(8,128)} %copy.18), calls=%async_computation | async-start | bytes 37748736 | tf_op jit(solution)/shard_map/all_to_all | solution.py:70
  666.3 13.1 %all-to-all-start.1 = ((f32[32,16,216]{2,0,1:T(8,128)}), f32[32,16,216]{2,0,1:T(8,128)}, u32[]{:S(2)}, u32[]{:S(2)}) async-start(f32[32,16,216]{2,0,1:T(8,128)} %copy.22), calls=%async_computation.1 | async-start | bytes 1048576 | tf_op jit(solution)/shard_map/all_to_all | solution.py:75
  679.3 18.1 %all-to-all-start.2 = ((f32[32,16,432]{2,0,1:T(8,128)}), f32[32,16,432]{2,0,1:T(8,128)S(1)}, u32[]{:S(2)}, u32[]{:S(2)}) async-start(f32[32,16,432]{2,0,1:T(8,128)} %copy.25), calls=%async_computation.2 | async-start | bytes 2097152 | tf_op jit(solution)/shard_map/all_to_all | solution.py:76
where the time goes:
time: 710 us; the launch traced here: 704 us
  waiting for transfers between devices  422 us (59%)
  matrix products  129 us (18%)
  other arithmetic  85.6 us (12%)
  local copies, waits for them, and re-layouts  51.1 us (7%)
  starting transfers between devices  15.1 us (2%)
    all_to_all x1, waiting for transfers between devices, on_device(): lax.all_to_all(merged, 'py', split_axis=0, concat_axis=1, tiled=True)  409 us
    dot_general x2, matrix products, filter_first(): jnp.einsum('fzyn,nk->kyfz', fields, circulant_taps(n_cells), precision=hi...  105 us
    unnamed x10, other arithmetic  63.3 us
    concatenate x1, local copies, waits for them, and re-layouts, on_device(): merged = jnp.concatenate([vel_first, prod_first], axis=2)  18 us
    dot_general x1, matrix products, filter_second(): jnp.einsum('kym,yj->kjm', moved, taps_matrix((y_total - 32) // 8), precis...  17.1 us
  transfers between devices with their start and end apart: 3, of which 3 were waited for; matrix products, arithmetic and copies ran while one was open for 1% of the time, Pallas kernels for 0%

commit v1 on v0

v1 whole, which is shorter than its diff:
```python
import functools
import numpy as np
import ml_dtypes
import jax
import jax.numpy as jnp
from jax import lax
from jax.sharding import PartitionSpec as P
from jax.experimental import pallas as pl
from jax.experimental.pallas import tpu as pltpu

stress_pairs = ((0, 0), (0, 1), (0, 2), (1, 1), (1, 2), (2, 2))
f32, bf16 = jnp.float32, jnp.bfloat16


def tap(t):
    r = np.arange(-16, 17).astype(np.float64)
    s = np.sum(np.exp(-r * r / 128.0))
    t = np.asarray(t, np.float64)
    return np.where(np.abs(t) <= 16, np.exp(-t * t / 128.0) / s, 0.0)


class Plan:
    def __init__(self, shape, npy, npz):
        _, self.zl, self.yl, self.nx = shape
        self.npy, self.npz = npy, npz
        zl, yl = self.zl, self.yl
        self.oz = (zl * npz - 32) // 8
        self.oy = (yl * npy - 32) // 8
        self.ox = self.nx // 8
        self.kb = self.ox // npy
        self.jq = self.oy // npz
        self.pk = 128 // self.kb
        self.cz = max(c for c in range(1, 9) if zl % c == 0)
        self.nch = zl // self.cz
        self.yp = -(-yl // 8) * 8
        self.kk = self.cz * self.yp
        cz, nch = self.cz, self.nch
        base = lambda s: (s + 7) // 8 - 4
        self.base_p = [base(zl * p) for p in range(npz)]
        starts = np.array([[zl * p + cz * c for c in range(nch)] for p in range(npz)])
        bases = base(starts)
        self.nic = int(np.max((starts + cz - 1) // 8 - bases + 1))
        self.offs = bases - bases[:, :1]
        self.ni = int(self.offs.max()) + self.nic
        self.groups = -(-self.ni // self.pk)
        z = starts[:, :, None, None] + np.arange(cz)[None, None, None, :]
        i = bases[:, :, None, None] + np.arange(8)[None, None, :, None]
        az = np.where((i >= 0) & (i < self.oz), tap(z - 16 - 8 * i), 0.0)
        az[:, :, self.nic:] = 0.0
        self.az = np.repeat(az, self.yp, axis=3).astype(np.float32)
        ay = np.zeros((npy, 8, self.yp))
        self.mask = np.zeros((npy, self.oy // 8, 8), np.float32)
        for d in range(npy):
            y = yl * d + np.arange(yl)
            for j in range(self.oy):
                w = tap(y - 16 - 8 * j)
                if np.any(w != 0):
                    ay[d, j % 8, :yl] += w
                    self.mask[d, j // 8, j % 8] = 1.0
        assert self.mask.sum(axis=1).max() == 1
        self.ay = np.tile(ay, (1, 1, cz)).astype(np.float32)
        n = np.arange(self.nx)[:, None]
        k = np.arange(self.ox)[None, :]
        t = (n - 8 * k + self.nx // 2) % self.nx - self.nx // 2
        wx = tap(t).astype(np.float32)
        self.wx_hi = wx.astype(ml_dtypes.bfloat16)
        self.wx_lo = (wx - self.wx_hi.astype(np.float32)).astype(ml_dtypes.bfloat16)


def split(val):
    hi = val.astype(bf16)
    return hi, (val - hi.astype(f32)).astype(bf16)


def dot(a, b):
    return jnp.dot(a, b, preferred_element_type=f32)


def sum_block(pn, c, p, d, v_ref, az_ref, ay_ref, acc):
    xt = 256
    wz = az_ref[p, c][: pn.nic]
    wy = ay_ref[d]
    w = (wz[:, None, :] * wy[None, :, :]).reshape(pn.nic * 8, pn.kk)
    w_hi = w.astype(bf16).astype(f32)
    w2 = jnp.concatenate([w_hi, w - w_hi], axis=0).astype(bf16)
    off = (pn.zl * p + pn.cz * c + 7) // 8 - (pn.zl * p + 7) // 8
    m = pn.nic * 8

    def tile(x, carry):
        xs = pl.ds(pl.multiple_of(x * xt, xt), xt)
        comps = []
        for a in range(3):
            blk = v_ref[a, :, :, xs]
            if pn.yp > pn.yl:
                blk = jnp.concatenate([blk, jnp.zeros((pn.cz, pn.yp - pn.yl, xt), f32)], axis=1)
            comps.append(blk.reshape(pn.kk, xt))
        for f in range(9):
            if f < 3:
                val = comps[f]
            else:
                a, b = stress_pairs[f - 3]
                val = comps[a] * comps[b]
            hi, lo = split(val)
            r = dot(w2, hi) + dot(w2, lo)
            r = (r[:m] + r[m:]).reshape(pn.nic, 8, xt)
            acc[f, pl.ds(off, pn.nic), :, xs] += r
        return carry

    lax.fori_loop(0, pn.nx // xt, tile, 0)


def first_group(pn, g, acc, wh_ref, wl_ref, out_ref):
    rows = min(pn.pk, pn.ni - g * pn.pk)
    parts = []
    for q in range(rows):
        a = acc[:, g * pn.pk + q].reshape(72, pn.nx)
        hi, lo = split(a)
        parts.append(dot(hi, wh_ref[...]) + (dot(lo, wh_ref[...]) + dot(hi, wl_ref[...])))
    lane = lax.broadcasted_iota(jnp.int32, (72, 128), 1)
    for m in range(pn.npy):
        mg, mo = divmod(m * pn.kb, 128)
        res = jnp.zeros((72, 128), f32)
        for q in range(rows):
            piece = parts[q][:, mg * 128:(mg + 1) * 128]
            shift = (q * pn.kb - mo) % 128
            if shift:
                piece = pltpu.roll(piece, shift, 1)
            res = jnp.where((lane >= q * pn.kb) & (lane < (q + 1) * pn.kb), piece, res)
        out_ref[m, g] = res.reshape(9, 8, 128)


def local_kernel(pn, v_ref, az_ref, ay_ref, wh_ref, wl_ref, out_ref, acc):
    c = pl.program_id(0)
    d, p = lax.axis_index("py"), lax.axis_index("pz")

    @pl.when(c == 0)
    def _():
        acc[...] = jnp.zeros_like(acc)

    sum_block(pn, c, p, d, v_ref, az_ref, ay_ref, acc)

    @pl.when(c == pn.nch - 1)
    def _():
        for g in range(pn.groups):
            first_group(pn, g, acc, wh_ref, wl_ref, out_ref)


def local_sums(pn, velocity):
    whole = lambda a: pl.BlockSpec(a.shape, lambda c: (0,) * a.ndim)
    tables = [pn.az, pn.ay, pn.wx_hi, pn.wx_lo]
    return pl.pallas_call(
        functools.partial(local_kernel, pn),
        grid=(pn.nch,),
        in_specs=[pl.BlockSpec((3, pn.cz, pn.yl, pn.nx), lambda c: (0, c, 0, 0))] + [whole(t) for t in tables],
        out_specs=pl.BlockSpec((pn.npy, pn.groups, 9, 8, 128), lambda c: (0, 0, 0, 0, 0)),
        out_shape=jax.ShapeDtypeStruct((pn.npy, pn.groups, 9, 8, 128), f32),
        scratch_shapes=[pltpu.VMEM((9, pn.ni, 8, pn.nx), f32)],
        compiler_params=pltpu.CompilerParams(vmem_limit_bytes=50 * 2**20),
    )(velocity, *[jnp.asarray(t) for t in tables])


def on_device(npy, npz, velocity):
    pn = Plan(velocity.shape, npy, npz)
    packed = local_sums(pn, velocity)
    moved = lax.all_to_all(packed, "py", split_axis=0, concat_axis=0, tiled=True)
    mask = pn.mask[:, :, None, None, :, None]
    rows = jnp.sum(jnp.where(mask > 0, moved[:, None], 0.0), axis=0)
    rows = jnp.transpose(rows, (0, 3, 1, 2, 4)).reshape(npz, pn.jq, pn.groups, 9, 128)
    planes = lax.all_to_all(rows, "pz", split_axis=0, concat_axis=0, tiled=True)
    planes = planes.reshape(npz, pn.jq, pn.groups, 9, pn.pk, pn.kb)
    planes = jnp.transpose(planes, (0, 3, 2, 4, 1, 5)).reshape(npz, 9, pn.groups * pn.pk, pn.jq, pn.kb)
    total = 0.0
    for p in range(npz):
        lo = pn.base_p[p]
        i0, i1 = max(lo, 0), min(lo + pn.ni, pn.oz)
        total = total + jnp.pad(
            planes[p][:, i0 - lo:i1 - lo], ((0, 0), (i0, pn.oz - i1), (0, 0), (0, 0))
        )
    stresses = jnp.stack([total[3 + n] - total[a] * total[b] for n, (a, b) in enumerate(stress_pairs)])
    return total[:3], stresses


def solution(mesh):
    return jax.shard_map(
        functools.partial(on_device, mesh.shape["py"], mesh.shape["pz"]),
        mesh=mesh,
        in_specs=(P(None, "pz", "py", None),),
        out_specs=(P(None, None, "pz", "py"), P(None, None, "pz", "py")),
        check_vma=False,
    )
```

time: 710 us -> 137 us (0.19)
  waiting for transfers between devices: 422 us -> 0 us
  matrix products: 129 us -> 0 us
  other arithmetic: 85.6 us -> 0.57 us
  Pallas kernels: 0 us -> 46.8 us
  blocking collectives: 0 us -> 45 us
  starting transfers between devices: 15.1 us -> 0 us
  local copies, waits for them, and re-layouts: 51.1 us -> 44 us
    all_to_all x3 -> x0, waiting for transfers between devices: 422 us -> none  [the longest x1 409 us: on_device(): lax.all_to_all(merged, 'py', split_axis=0, concat_axis=1, tiled=True)]
    dot_general x5 -> x0, matrix products: 129 us -> none  [the longest x2 105 us: filter_first(): jnp.einsum('fzyn,nk->kyfz', fields, circulant_taps(n_cells), precision=hi...]
    unnamed x10 -> x5, other arithmetic: 63.3 us -> 0.15 us
    pallas_call x0 -> x1, Pallas kernels: none -> 46.8 us  [local_sums(): pl.pallas_call(functools.partial(local_kernel, pn), grid=(pn.nch,), in_sp...]
    all_to_all x0 -> x2, blocking collectives: none -> 45 us  [the longest x1 36 us: on_device(): lax.all_to_all(packed, 'py', split_axis=0, concat_axis=0, tiled=True)]
    unnamed x2 -> x17, local copies, waits for them, and re-layouts: 1.81 us -> 42.3 us
    concatenate x1 -> x0, local copies, waits for them, and re-layouts: 18 us -> none  [on_device(): merged = jnp.concatenate([vel_first, prod_first], axis=2)]
    all_to_all x3 -> x0, starting transfers between devices: 15.1 us -> none  [the longest x1 7.25 us: on_device(): lax.all_to_all(merged, 'py', split_axis=0, concat_axis=1, tiled=True)]
  transfers between devices with their start and end apart: 3 -> 0, of which waited for: 3 -> 0; matrix products, arithmetic and copies ran while one was open for 1% -> 0% of each run, Pallas kernels for 0% -> 0%
where the time goes in v1:
time: 137 us
  Pallas kernels  46.8 us (34%)
  blocking collectives  45 us (33%)
  local copies, waits for them, and re-layouts  44 us (32%)
    pallas_call x1, Pallas kernels, local_sums(): pl.pallas_call(functools.partial(local_kernel, pn), grid=(pn.nch,), in_sp...  46.8 us
    unnamed x17, local copies, waits for them, and re-layouts  42.3 us
    all_to_all x1, blocking collectives, on_device(): lax.all_to_all(packed, 'py', split_axis=0, concat_axis=0, tiled=True)  36 us
    all_to_all x1, blocking collectives, on_device(): planes = lax.all_to_all(rows, 'pz', split_axis=0, concat_axis=0, tiled=True)  8.98 us

profile of v1, /device:TPU:0, one launch (start us, length us, event | category | flops | bytes accessed | tf_op | source)
XLA Modules:
  0.0 137.2 jit_solution(6135584958745479670)
XLA Ops:
  0.6 0.0 copy-start
  0.6 0.0 copy-start.1
  0.7 0.0 copy-start.2
  0.7 0.0 copy-start.3
  0.7 41.2 %copy.22.v_ref = f32[3,72,20,2048]{3,2,1,0:T(8,128)} copy(f32[3,72,20,2048]{3,1,2,0:T(8,128)} %param.6) | data formatting | bytes 70778880 | tf_op args[0]
  41.9 0.0 copy-done
  41.9 0.0 copy-done.1
  41.9 0.0 copy-done.2
  41.9 0.0 copy-done.3
  41.9 46.8 %shard_map.77 = f32[8,4,9,8,128]{4,3,2,1,0:T(8,128)S(1)} custom-call(f32[3,72,20,2048]{3,2,1,0:T(8,128)} %copy.22.v_ref, f32[4,9,8,192]{3,2,1,0:T(8,128)S(1)} %copy-done.2, f32[8,8,192]{2,1,0:T(8,128)S(1)} %copy-done.3, bf16[2048,256]{1,0:T(8,128)(2,1)S(1)} %copy-done.1, bf16[2048,256]{1,0:T(8,128)(2,1)S(1)} %copy-done), custom_call_target="tpu_custom_call" | custom-call | tf_op jit(solution)/shard_map/pallas_call | solution.py:151
  88.7 0.0 copy-start.5
  88.8 36.0 %all_to_all.10 = f32[8,4,9,8,128]{4,3,2,1,0:T(8,128)S(1)} all-to-all(f32[8,4,9,8,128]{4,3,2,1,0:T(8,128)S(1)} %shard_map.77), channel_id=1, replica_groups=mesh['py'=8,'pz'=4] {'py'}, dimensions={0} | all-to-all | bytes 2359296 | tf_op jit(solution)/shard_map/all_to_all | solution.py:165
  124.8 0.0 copy-done.5
  124.8 0.2 select_reduce_fusion
  125.0 0.1 copy.24
  125.1 9.0 %all_to_all.11 = f32[4,4,4,9,128]{4,1,3,2,0:T(4,128)S(1)} all-to-all(f32[4,4,4,9,128]{4,1,3,2,0:T(4,128)S(1)} %copy.24), channel_id=1, replica_groups=mesh['py'=8,'pz'=4] {'pz'}, dimensions={0} | all-to-all | bytes 589824 | tf_op jit(solution)/shard_map/all_to_all | solution.py:169
  134.1 0.1 copy.25
  134.1 0.6 reshape.21
  134.7 0.2 fusion.6
  135.0 0.1 copy.30
  135.1 0.1 copy.33
  135.1 0.1 copy.32
  135.2 0.1 copy.31
  135.3 0.2 pad_add_fusion
  135.5 0.7 slice.93
  136.4 0.0 copy-start.4
  136.4 0.7 copy-done.4
  (8 shorter events, 0.2 us)
Async XLA Ops:
  0.6 41.3 %copy-start = (bf16[2048,256]{1,0:T(8,128)(2,1)S(1)}, bf16[2048,256]{1,0:T(8,128)(2,1)}, u32[]{:S(2)}) copy-start(bf16[2048,256]{1,0:T(8,128)(2,1)} %constant.17.clone.wl_ref) | copy-start | bytes 3145732
  0.6 41.3 %copy-start.1 = (bf16[2048,256]{1,0:T(8,128)(2,1)S(1)}, bf16[2048,256]{1,0:T(8,128)(2,1)}, u32[]{:S(2)}) copy-start(bf16[2048,256]{1,0:T(8,128)(2,1)} %constant.16.clone.wh_ref) | copy-start | bytes 3145732
  0.7 41.3 %copy-start.2 = (f32[4,9,8,192]{3,2,1,0:T(8,128)S(1)}, f32[4,9,8,192]{3,2,1,0:T(8,128)}, u32[]{:S(2)}) copy-start(f32[4,9,8,192]{3,2,1,0:T(8,128)} %constant.14.clone.az_ref) | copy-start | bytes 663556
  0.7 41.3 %copy-start.3 = (f32[8,8,192]{2,1,0:T(8,128)S(1)}, f32[8,8,192]{2,1,0:T(8,128)}, u32[]{:S(2)}) copy-start(f32[8,8,192]{2,1,0:T(8,128)} %constant.15.clone.ay_ref) | copy-start | bytes 147460
  88.7 36.0 %copy-start.5 = (pred[8,2,8]{2,1,0:T(4,128)(4,1)S(1)}, pred[8,2,8]{2,1,0:T(4,128)(4,1)}, u32[]{:S(2)}) copy-start(pred[8,2,8]{2,1,0:T(4,128)(4,1)} %constant.28) | copy-start | bytes 388
  136.4 0.7 copy-start.4

commit v2 on v1

--- a/solution.py
+++ b/solution.py
@@ -30,10 +30,10 @@
         self.kb = self.ox // npy
         self.jq = self.oy // npz
         self.pk = 128 // self.kb
-        self.cz = max(c for c in range(1, 9) if zl % c == 0)
+        self.cz = 8 if zl % 8 == 0 else zl
         self.nch = zl // self.cz
-        self.yp = -(-yl // 8) * 8
-        self.kk = self.cz * self.yp
+        self.zp = -(-self.cz // 8) * 8
+        self.kk = yl * self.zp
         cz, nch = self.cz, self.nch
         base = lambda s: (s + 7) // 8 - 4
         self.base_p = [base(zl * p) for p in range(npz)]
@@ -47,18 +47,19 @@
         i = bases[:, :, None, None] + np.arange(8)[None, None, :, None]
         az = np.where((i >= 0) & (i < self.oz), tap(z - 16 - 8 * i), 0.0)
         az[:, :, self.nic:] = 0.0
-        self.az = np.repeat(az, self.yp, axis=3).astype(np.float32)
-        ay = np.zeros((npy, 8, self.yp))
+        az = np.pad(az, ((0, 0), (0, 0), (0, 0), (0, self.zp - cz)))
+        self.az = np.tile(az, (1, 1, 1, yl)).astype(np.float32)
+        ay = np.zeros((npy, 8, yl))
         self.mask = np.zeros((npy, self.oy // 8, 8), np.float32)
         for d in range(npy):
             y = yl * d + np.arange(yl)
             for j in range(self.oy):
                 w = tap(y - 16 - 8 * j)
                 if np.any(w != 0):
-                    ay[d, j % 8, :yl] += w
+                    ay[d, j % 8] += w
                     self.mask[d, j // 8, j % 8] = 1.0
         assert self.mask.sum(axis=1).max() == 1
-        self.ay = np.tile(ay, (1, 1, cz)).astype(np.float32)
+        self.ay = np.repeat(ay, self.zp, axis=2).astype(np.float32)
         n = np.arange(self.nx)[:, None]
         k = np.arange(self.ox)[None, :]
         t = (n - 8 * k + self.nx // 2) % self.nx - self.nx // 2
@@ -91,8 +92,8 @@
         comps = []
         for a in range(3):
             blk = v_ref[a, :, :, xs]
-            if pn.yp > pn.yl:
-                blk = jnp.concatenate([blk, jnp.zeros((pn.cz, pn.yp - pn.yl, xt), f32)], axis=1)
+            if pn.zp > pn.cz:
+                blk = jnp.concatenate([blk, jnp.zeros((pn.yl, pn.zp - pn.cz, xt), f32)], axis=1)
             comps.append(blk.reshape(pn.kk, xt))
         for f in range(9):
             if f < 3:
@@ -151,7 +152,7 @@
     return pl.pallas_call(
         functools.partial(local_kernel, pn),
         grid=(pn.nch,),
-        in_specs=[pl.BlockSpec((3, pn.cz, pn.yl, pn.nx), lambda c: (0, c, 0, 0))] + [whole(t) for t in tables],
+        in_specs=[pl.BlockSpec((3, pn.yl, pn.cz, pn.nx), lambda c: (0, 0, c, 0))] + [whole(t) for t in tables],
         out_specs=pl.BlockSpec((pn.npy, pn.groups, 9, 8, 128), lambda c: (0, 0, 0, 0, 0)),
         out_shape=jax.ShapeDtypeStruct((pn.npy, pn.groups, 9, 8, 128), f32),
         scratch_shapes=[pltpu.VMEM((9, pn.ni, 8, pn.nx), f32)],
@@ -161,7 +162,7 @@
 
 def on_device(npy, npz, velocity):
     pn = Plan(velocity.shape, npy, npz)
-    packed = local_sums(pn, velocity)
+    packed = local_sums(pn, jnp.transpose(velocity, (0, 2, 1, 3)))
     moved = lax.all_to_all(packed, "py", split_axis=0, concat_axis=0, tiled=True)
     mask = pn.mask[:, :, None, None, :, None]
     rows = jnp.sum(jnp.where(mask > 0, moved[:, None], 0.0), axis=0)

time: 137 us -> 92.4 us (0.67)
  local copies, waits for them, and re-layouts: 44 us -> 7 us
  Pallas kernels: 46.8 us -> 38.7 us
    unnamed x17 -> x16, local copies, waits for them, and re-layouts: 42.3 us -> 5.32 us
    pallas_call x1, Pallas kernels: 46.8 us -> 38.7 us  [local_sums(): pl.pallas_call(functools.partial(local_kernel, pn), grid=(pn.nch,), in_sp...]
where the time goes in v2:
time: 92.4 us; the launch traced here: 92.1 us
  blocking collectives  45 us (49%)
  Pallas kernels  38.7 us (42%)
  local copies, waits for them, and re-layouts  7 us (8%)
    pallas_call x1, Pallas kernels, local_sums(): pl.pallas_call(functools.partial(local_kernel, pn), grid=(pn.nch,), in_sp...  38.7 us
    all_to_all x1, blocking collectives, on_device(): lax.all_to_all(packed, 'py', split_axis=0, concat_axis=0, tiled=True)  36 us
    all_to_all x1, blocking collectives, on_device(): planes = lax.all_to_all(rows, 'pz', split_axis=0, concat_axis=0, tiled=True)  8.99 us
    unnamed x16, local copies, waits for them, and re-layouts  5.32 us

profile of v2, /device:TPU:0, one launch (start us, length us, event | category | flops | bytes accessed | tf_op | source)
XLA Modules:
  0.0 92.1 jit_solution(12962913132696759942)
XLA Ops:
  0.6 0.0 copy-start
  0.6 1.2 %copy-done = bf16[2048,256]{1,0:T(8,128)(2,1)S(1)} copy-done((bf16[2048,256]{1,0:T(8,128)(2,1)S(1)}, bf16[2048,256]{1,0:T(8,128)(2,1)}, u32[]{:S(2)}) %copy-start) | copy-done | bytes 1048600
  1.9 0.0 copy-start.1
  1.9 1.2 %copy-done.1 = bf16[2048,256]{1,0:T(8,128)(2,1)S(1)} copy-done((bf16[2048,256]{1,0:T(8,128)(2,1)S(1)}, bf16[2048,256]{1,0:T(8,128)(2,1)}, u32[]{:S(2)}) %copy-start.1) | copy-done | bytes 1048600
  3.1 0.0 copy-start.2
  3.1 1.0 %copy-done.2 = f32[4,9,8,160]{3,2,1,0:T(8,128)S(1)} copy-done((f32[4,9,8,160]{3,2,1,0:T(8,128)S(1)}, f32[4,9,8,160]{3,2,1,0:T(8,128)}, u32[]{:S(2)}) %copy-start.2) | copy-done | bytes 184344
  4.0 0.0 copy-start.3
  4.0 0.8 copy-done.3
  4.9 38.7 %shard_map.77 = f32[8,4,9,8,128]{4,3,2,1,0:T(8,128)S(1)} custom-call(f32[3,20,72,2048]{3,2,1,0:T(8,128)} %bitcast.13, f32[4,9,8,160]{3,2,1,0:T(8,128)S(1)} %copy-done.2, f32[8,8,160]{2,1,0:T(8,128)S(1)} %copy-done.3, bf16[2048,256]{1,0:T(8,128)(2,1)S(1)} %copy-done.1, bf16[2048,256]{1,0:T(8,128)(2,1)S(1)} %copy-done), custom_call_target="tpu_custom_call" | custom-call | tf_op jit(solution)/shard_map/pallas_call | solution.py:152
  43.6 0.0 copy-start.5
  43.6 36.0 %all_to_all.10 = f32[8,4,9,8,128]{4,3,2,1,0:T(8,128)S(1)} all-to-all(f32[8,4,9,8,128]{4,3,2,1,0:T(8,128)S(1)} %shard_map.77), channel_id=1, replica_groups=mesh['py'=8,'pz'=4] {'py'}, dimensions={0} | all-to-all | bytes 2359296 | tf_op jit(solution)/shard_map/all_to_all | solution.py:166
  79.6 0.0 copy-done.5
  79.6 0.2 select_reduce_fusion
  79.9 0.1 copy.20
  80.0 9.0 %all_to_all.11 = f32[4,4,4,9,128]{4,1,3,2,0:T(4,128)S(1)} all-to-all(f32[4,4,4,9,128]{4,1,3,2,0:T(4,128)S(1)} %copy.20), channel_id=1, replica_groups=mesh['py'=8,'pz'=4] {'pz'}, dimensions={0} | all-to-all | bytes 589824 | tf_op jit(solution)/shard_map/all_to_all | solution.py:170
  88.9 0.1 copy.21
  89.0 0.6 reshape.21
  89.6 0.2 fusion.6
  89.9 0.1 copy.26
  90.0 0.1 copy.29
  90.0 0.1 copy.28
  90.1 0.1 copy.27
  90.2 0.2 pad_add_fusion
  90.4 0.7 slice.93
  91.3 0.0 copy-start.4
  91.3 0.7 copy-done.4
  (8 shorter events, 0.2 us)
Async XLA Ops:
  0.6 1.2 %copy-start = (bf16[2048,256]{1,0:T(8,128)(2,1)S(1)}, bf16[2048,256]{1,0:T(8,128)(2,1)}, u32[]{:S(2)}) copy-start(bf16[2048,256]{1,0:T(8,128)(2,1)} %constant.17.clone.wl_ref) | copy-start | bytes 3145732
  1.9 1.2 %copy-start.1 = (bf16[2048,256]{1,0:T(8,128)(2,1)S(1)}, bf16[2048,256]{1,0:T(8,128)(2,1)}, u32[]{:S(2)}) copy-start(bf16[2048,256]{1,0:T(8,128)(2,1)} %constant.16.clone.wh_ref) | copy-start | bytes 3145732
  3.1 1.0 %copy-start.2 = (f32[4,9,8,160]{3,2,1,0:T(8,128)S(1)}, f32[4,9,8,160]{3,2,1,0:T(8,128)}, u32[]{:S(2)}) copy-start(f32[4,9,8,160]{3,2,1,0:T(8,128)} %constant.14.clone.az_ref) | copy-start | bytes 552964
  4.0 0.8 copy-start.3
  43.6 36.0 %copy-start.5 = (pred[8,2,8]{2,1,0:T(4,128)(4,1)S(1)}, pred[8,2,8]{2,1,0:T(4,128)(4,1)}, u32[]{:S(2)}) copy-start(pred[8,2,8]{2,1,0:T(4,128)(4,1)} %constant.28) | copy-start | bytes 388
  91.3 0.7 copy-start.4

commit v3 on v2

--- a/solution.py
+++ b/solution.py
@@ -160,25 +160,86 @@
     )(velocity, *[jnp.asarray(t) for t in tables])
 
 
+def exchange_kernel(pn, in_ref, vel_ref, str_ref, rec_y, snd_z, rec_z, sy, ry, sz, rz):
+    d, p = lax.axis_index("py"), lax.axis_index("pz")
+    npy, npz, jq, kb = pn.npy, pn.npz, pn.jq, pn.kb
+    mesh_id = pl.DeviceIdType.MESH
+    barrier = pltpu.get_barrier_semaphore()
+    for o in range(1, npy):
+        pl.semaphore_signal(barrier, inc=1, device_id=(lax.rem(d + o, npy), p), device_id_type=mesh_id)
+    for o in range(1, npz):
+        pl.semaphore_signal(barrier, inc=1, device_id=(d, lax.rem(p + o, npz)), device_id_type=mesh_id)
+    pl.semaphore_wait(barrier, npy + npz - 2)
+
+    copies = []
+    for o in range(1, npy):
+        to = lax.rem(d + o, npy)
+        copies.append(pltpu.make_async_remote_copy(
+            src_ref=in_ref.at[to], dst_ref=rec_y.at[d], send_sem=sy.at[o], recv_sem=ry.at[o],
+            device_id=(to, p), device_id_type=mesh_id))
+        copies[-1].start()
+    rec_y[d] = in_ref[d]
+    for copy in copies:
+        copy.wait()
+
+    row = lax.broadcasted_iota(jnp.int32, (9, 8, 128), 1)
+    for g in range(pn.groups):
+        for h in range(pn.oy // 8):
+            total = jnp.zeros((9, 8, 128), f32)
+            for s in range(npy):
+                rows = np.nonzero(pn.mask[s, h])[0]
+                if len(rows) == 0:
+                    continue
+                val = rec_y[s, g]
+                if len(rows) < 8:
+                    val = jnp.where((row >= int(rows[0])) & (row <= int(rows[-1])), val, 0.0)
+                total = total + val
+            for part in range(8 // jq):
+                snd_z[h * (8 // jq) + part, g] = total[:, part * jq:(part + 1) * jq, :]
+
+    copies = []
+    for o in range(1, npz):
+        to = lax.rem(p + o, npz)
+        copies.append(pltpu.make_async_remote_copy(
+            src_ref=snd_z.at[to], dst_ref=rec_z.at[p], send_sem=sz.at[o], recv_sem=rz.at[o],
+            device_id=(d, to), device_id_type=mesh_id))
+        copies[-1].start()
+    rec_z[p] = snd_z[p]
+    for copy in copies:
+        copy.wait()
+
+    for i in range(pn.oz):
+        total = jnp.zeros((9, jq, kb), f32)
+        for s in range(npz):
+            n = i - pn.base_p[s]
+            if 0 <= n < pn.ni:
+                g, q = divmod(n, pn.pk)
+                total = total + rec_z[s, g, :, :, q * kb:(q + 1) * kb]
+        vel_ref[:, i] = total[:3]
+        for n, (a, b) in enumerate(stress_pairs):
+            str_ref[n, i] = total[3 + n] - total[a] * total[b]
+
+
+def exchange(pn, packed):
+    vmem = pl.BlockSpec(memory_space=pltpu.VMEM)
+    zbuf = pltpu.VMEM((pn.npz, pn.groups, 9, pn.jq, 128), f32)
+    sems = [pltpu.SemaphoreType.DMA((n,)) for n in (pn.npy, pn.npy, pn.npz, pn.npz)]
+    return pl.pallas_call(
+        functools.partial(exchange_kernel, pn),
+        in_specs=[vmem],
+        out_specs=(vmem, vmem),
+        out_shape=tuple(jax.ShapeDtypeStruct((n, pn.oz, pn.jq, pn.kb), f32) for n in (3, 6)),
+        scratch_shapes=[pltpu.VMEM((pn.npy, pn.groups, 9, 8, 128), f32), zbuf, zbuf] + sems,
+        compiler_params=pltpu.CompilerParams(
+            collective_id=0, has_side_effects=True, vmem_limit_bytes=32 * 2**20
+        ),
+    )(packed)
+
+
 def on_device(npy, npz, velocity):
     pn = Plan(velocity.shape, npy, npz)
     packed = local_sums(pn, jnp.transpose(velocity, (0, 2, 1, 3)))
-    moved = lax.all_to_all(packed, "py", split_axis=0, concat_axis=0, tiled=True)
-    mask = pn.mask[:, :, None, None, :, None]
-    rows = jnp.sum(jnp.where(mask > 0, moved[:, None], 0.0), axis=0)
-    rows = jnp.transpose(rows, (0, 3, 1, 2, 4)).reshape(npz, pn.jq, pn.groups, 9, 128)
-    planes = lax.all_to_all(rows, "pz", split_axis=0, concat_axis=0, tiled=True)
-    planes = planes.reshape(npz, pn.jq, pn.groups, 9, pn.pk, pn.kb)
-    planes = jnp.transpose(planes, (0, 3, 2, 4, 1, 5)).reshape(npz, 9, pn.groups * pn.pk, pn.jq, pn.kb)
-    total = 0.0
-    for p in range(npz):
-        lo = pn.base_p[p]
-        i0, i1 = max(lo, 0), min(lo + pn.ni, pn.oz)
-        total = total + jnp.pad(
-            planes[p][:, i0 - lo:i1 - lo], ((0, 0), (i0, pn.oz - i1), (0, 0), (0, 0))
-        )
-    stresses = jnp.stack([total[3 + n] - total[a] * total[b] for n, (a, b) in enumerate(stress_pairs)])
-    return total[:3], stresses
+    return exchange(pn, packed)
 
 
 def solution(mesh):

time: 92.4 us -> 81.7 us (0.88)
  the two profiles are of different devices: /device:TPU:0 before, /device:TPU:11 now
where the time goes in v3:
time: 81.7 us; the launch traced here: 81.5 us
  Pallas kernels  75.1 us (92%)
  local copies, waits for them, and re-layouts  5.67 us (7%)
    pallas_call x1, Pallas kernels, local_sums(): pl.pallas_call(functools.partial(local_kernel, pn), grid=(pn.nch,), in_sp...  38.7 us
    pallas_call x1, Pallas kernels, exchange(): pl.pallas_call(functools.partial(exchange_kernel, pn), in_specs=[vmem], o...  36.4 us
    unnamed x10, local copies, waits for them, and re-layouts  5.67 us

profile of v3, /device:TPU:11, one launch (start us, length us, event | category | flops | bytes accessed | tf_op | source)
XLA Modules:
  0.0 81.5 jit_solution(8838897915565139115)
XLA Ops:
  0.6 0.0 copy-start
  0.6 1.2 %copy-done = bf16[2048,256]{1,0:T(8,128)(2,1)S(1)} copy-done((bf16[2048,256]{1,0:T(8,128)(2,1)S(1)}, bf16[2048,256]{1,0:T(8,128)(2,1)}, u32[]{:S(2)}) %copy-start) | copy-done | bytes 1048600
  1.9 0.0 copy-start.1
  1.9 1.2 %copy-done.1 = bf16[2048,256]{1,0:T(8,128)(2,1)S(1)} copy-done((bf16[2048,256]{1,0:T(8,128)(2,1)S(1)}, bf16[2048,256]{1,0:T(8,128)(2,1)}, u32[]{:S(2)}) %copy-start.1) | copy-done | bytes 1048600
  3.1 0.0 copy-start.2
  3.1 1.0 %copy-done.2 = f32[4,9,8,160]{3,2,1,0:T(8,128)S(1)} copy-done((f32[4,9,8,160]{3,2,1,0:T(8,128)S(1)}, f32[4,9,8,160]{3,2,1,0:T(8,128)}, u32[]{:S(2)}) %copy-start.2) | copy-done | bytes 184344
  4.0 0.0 copy-start.3
  4.0 0.8 %copy-done.3 = f32[8,8,160]{2,1,0:T(8,128)S(1)} copy-done((f32[8,8,160]{2,1,0:T(8,128)S(1)}, f32[8,8,160]{2,1,0:T(8,128)}, u32[]{:S(2)}) %copy-start.3) | copy-done | bytes 40984
  4.9 38.7 %shard_map.68.in_ref = f32[8,4,9,8,128]{4,3,2,1,0:T(8,128)S(1)} custom-call(f32[3,20,72,2048]{3,2,1,0:T(8,128)} %bitcast.1, f32[4,9,8,160]{3,2,1,0:T(8,128)S(1)} %copy-done.2, f32[8,8,160]{2,1,0:T(8,128)S(1)} %copy-done.3, bf16[2048,256]{1,0:T(8,128)(2,1)S(1)} %copy-done.1, bf16[2048,256]{1,0:T(8,128)(2,1)S(1)} %copy-done), custom_call_target="tpu_custom_call" | custom-call | tf_op jit(solution)/shard_map/pallas_call | solution.py:152
  43.6 36.4 %shard_map.69 = (f32[3,32,4,32]{3,2,1,0:T(4,128)S(1)}, f32[6,32,4,32]{3,2,1,0:T(4,128)S(1)}) custom-call(f32[8,4,9,8,128]{4,3,2,1,0:T(8,128)S(1)} %shard_map.68.in_ref), custom_call_target="tpu_custom_call" | custom-call | tf_op jit(solution)/shard_map/pallas_call | solution.py:227
  80.0 0.7 copy.9
  80.7 0.7 copy.10
Async XLA Ops:
  0.6 1.2 %copy-start = (bf16[2048,256]{1,0:T(8,128)(2,1)S(1)}, bf16[2048,256]{1,0:T(8,128)(2,1)}, u32[]{:S(2)}) copy-start(bf16[2048,256]{1,0:T(8,128)(2,1)} %constant.11.clone.wl_ref) | copy-start | bytes 3145732
  1.9 1.2 %copy-start.1 = (bf16[2048,256]{1,0:T(8,128)(2,1)S(1)}, bf16[2048,256]{1,0:T(8,128)(2,1)}, u32[]{:S(2)}) copy-start(bf16[2048,256]{1,0:T(8,128)(2,1)} %constant.10.clone.wh_ref) | copy-start | bytes 3145732
  3.1 1.0 %copy-start.2 = (f32[4,9,8,160]{3,2,1,0:T(8,128)S(1)}, f32[4,9,8,160]{3,2,1,0:T(8,128)}, u32[]{:S(2)}) copy-start(f32[4,9,8,160]{3,2,1,0:T(8,128)} %constant.8.clone.az_ref) | copy-start | bytes 552964
  4.0 0.8 %copy-start.3 = (f32[8,8,160]{2,1,0:T(8,128)S(1)}, f32[8,8,160]{2,1,0:T(8,128)}, u32[]{:S(2)}) copy-start(f32[8,8,160]{2,1,0:T(8,128)} %constant.9.clone.ay_ref) | copy-start | bytes 122884

commit v4 on v3

--- a/solution.py
+++ b/solution.py
@@ -171,19 +171,23 @@
         pl.semaphore_signal(barrier, inc=1, device_id=(d, lax.rem(p + o, npz)), device_id_type=mesh_id)
     pl.semaphore_wait(barrier, npy + npz - 2)
 
-    copies = []
-    for o in range(1, npy):
-        to = lax.rem(d + o, npy)
-        copies.append(pltpu.make_async_remote_copy(
-            src_ref=in_ref.at[to], dst_ref=rec_y.at[d], send_sem=sy.at[o], recv_sem=ry.at[o],
-            device_id=(to, p), device_id_type=mesh_id))
-        copies[-1].start()
+    y_copies = []
+    for g in range(pn.groups):
+        y_copies.append([])
+        for o in range(1, npy):
+            to = lax.rem(d + o, npy)
+            copy = pltpu.make_async_remote_copy(
+                src_ref=in_ref.at[to, g], dst_ref=rec_y.at[d, g], send_sem=sy.at[g, o], recv_sem=ry.at[g, o],
+                device_id=(to, p), device_id_type=mesh_id)
+            copy.start()
+            y_copies[g].append(copy)
     rec_y[d] = in_ref[d]
-    for copy in copies:
-        copy.wait()
+    z_copies = []
 
     row = lax.broadcasted_iota(jnp.int32, (9, 8, 128), 1)
     for g in range(pn.groups):
+        for copy in y_copies[g]:
+            copy.wait()
         for h in range(pn.oy // 8):
             total = jnp.zeros((9, 8, 128), f32)
             for s in range(npy):
@@ -196,16 +200,15 @@
                 total = total + val
             for part in range(8 // jq):
                 snd_z[h * (8 // jq) + part, g] = total[:, part * jq:(part + 1) * jq, :]
-
-    copies = []
-    for o in range(1, npz):
-        to = lax.rem(p + o, npz)
-        copies.append(pltpu.make_async_remote_copy(
-            src_ref=snd_z.at[to], dst_ref=rec_z.at[p], send_sem=sz.at[o], recv_sem=rz.at[o],
-            device_id=(d, to), device_id_type=mesh_id))
-        copies[-1].start()
+        for o in range(1, npz):
+            to = lax.rem(p + o, npz)
+            copy = pltpu.make_async_remote_copy(
+                src_ref=snd_z.at[to, g], dst_ref=rec_z.at[p, g], send_sem=sz.at[g, o], recv_sem=rz.at[g, o],
+                device_id=(d, to), device_id_type=mesh_id)
+            copy.start()
+            z_copies.append(copy)
     rec_z[p] = snd_z[p]
-    for copy in copies:
+    for copy in z_copies:
         copy.wait()
 
     for i in range(pn.oz):
@@ -223,7 +226,7 @@
 def exchange(pn, packed):
     vmem = pl.BlockSpec(memory_space=pltpu.VMEM)
     zbuf = pltpu.VMEM((pn.npz, pn.groups, 9, pn.jq, 128), f32)
-    sems = [pltpu.SemaphoreType.DMA((n,)) for n in (pn.npy, pn.npy, pn.npz, pn.npz)]
+    sems = [pltpu.SemaphoreType.DMA((pn.groups, n)) for n in (pn.npy, pn.npy, pn.npz, pn.npz)]
     return pl.pallas_call(
         functools.partial(exchange_kernel, pn),
         in_specs=[vmem],

time: 81.7 us -> 80.9 us (level)
  the two profiles are of different devices: /device:TPU:11 before, /device:TPU:0 now
where the time goes in v4:
time: 80.9 us; the launch traced here: 80.6 us
  Pallas kernels  74.3 us (92%)
  local copies, waits for them, and re-layouts  5.67 us (7%)
    pallas_call x1, Pallas kernels, local_sums(): pl.pallas_call(functools.partial(local_kernel, pn), grid=(pn.nch,), in_sp...  38.7 us
    pallas_call x1, Pallas kernels, exchange(): pl.pallas_call(functools.partial(exchange_kernel, pn), in_specs=[vmem], o...  35.6 us
    unnamed x10, local copies, waits for them, and re-layouts  5.67 us

profile of v4, /device:TPU:0, one launch (start us, length us, event | category | flops | bytes accessed | tf_op | source)
XLA Modules:
  0.0 80.6 jit_solution(2095785353716288365)
XLA Ops:
  0.6 0.0 copy-start
  0.6 1.2 %copy-done = bf16[2048,256]{1,0:T(8,128)(2,1)S(1)} copy-done((bf16[2048,256]{1,0:T(8,128)(2,1)S(1)}, bf16[2048,256]{1,0:T(8,128)(2,1)}, u32[]{:S(2)}) %copy-start) | copy-done | bytes 1048600
  1.9 0.0 copy-start.1
  1.9 1.2 %copy-done.1 = bf16[2048,256]{1,0:T(8,128)(2,1)S(1)} copy-done((bf16[2048,256]{1,0:T(8,128)(2,1)S(1)}, bf16[2048,256]{1,0:T(8,128)(2,1)}, u32[]{:S(2)}) %copy-start.1) | copy-done | bytes 1048600
  3.1 0.0 copy-start.2
  3.1 1.0 %copy-done.2 = f32[4,9,8,160]{3,2,1,0:T(8,128)S(1)} copy-done((f32[4,9,8,160]{3,2,1,0:T(8,128)S(1)}, f32[4,9,8,160]{3,2,1,0:T(8,128)}, u32[]{:S(2)}) %copy-start.2) | copy-done | bytes 184344
  4.0 0.0 copy-start.3
  4.0 0.8 %copy-done.3 = f32[8,8,160]{2,1,0:T(8,128)S(1)} copy-done((f32[8,8,160]{2,1,0:T(8,128)S(1)}, f32[8,8,160]{2,1,0:T(8,128)}, u32[]{:S(2)}) %copy-start.3) | copy-done | bytes 40984
  4.9 38.7 %shard_map.68.in_ref = f32[8,4,9,8,128]{4,3,2,1,0:T(8,128)S(1)} custom-call(f32[3,20,72,2048]{3,2,1,0:T(8,128)} %bitcast.1, f32[4,9,8,160]{3,2,1,0:T(8,128)S(1)} %copy-done.2, f32[8,8,160]{2,1,0:T(8,128)S(1)} %copy-done.3, bf16[2048,256]{1,0:T(8,128)(2,1)S(1)} %copy-done.1, bf16[2048,256]{1,0:T(8,128)(2,1)S(1)} %copy-done), custom_call_target="tpu_custom_call" | custom-call | tf_op jit(solution)/shard_map/pallas_call | solution.py:152
  43.6 35.6 %shard_map.69 = (f32[3,32,4,32]{3,2,1,0:T(4,128)S(1)}, f32[6,32,4,32]{3,2,1,0:T(4,128)S(1)}) custom-call(f32[8,4,9,8,128]{4,3,2,1,0:T(8,128)S(1)} %shard_map.68.in_ref), custom_call_target="tpu_custom_call" | custom-call | tf_op jit(solution)/shard_map/pallas_call | solution.py:230
  79.2 0.7 copy.9
  79.9 0.7 copy.10
Async XLA Ops:
  0.6 1.2 %copy-start = (bf16[2048,256]{1,0:T(8,128)(2,1)S(1)}, bf16[2048,256]{1,0:T(8,128)(2,1)}, u32[]{:S(2)}) copy-start(bf16[2048,256]{1,0:T(8,128)(2,1)} %constant.11.clone.wl_ref) | copy-start | bytes 3145732
  1.9 1.2 %copy-start.1 = (bf16[2048,256]{1,0:T(8,128)(2,1)S(1)}, bf16[2048,256]{1,0:T(8,128)(2,1)}, u32[]{:S(2)}) copy-start(bf16[2048,256]{1,0:T(8,128)(2,1)} %constant.10.clone.wh_ref) | copy-start | bytes 3145732
  3.1 1.0 %copy-start.2 = (f32[4,9,8,160]{3,2,1,0:T(8,128)S(1)}, f32[4,9,8,160]{3,2,1,0:T(8,128)}, u32[]{:S(2)}) copy-start(f32[4,9,8,160]{3,2,1,0:T(8,128)} %constant.8.clone.az_ref) | copy-start | bytes 552964
  4.0 0.8 %copy-start.3 = (f32[8,8,160]{2,1,0:T(8,128)S(1)}, f32[8,8,160]{2,1,0:T(8,128)}, u32[]{:S(2)}) copy-start(f32[8,8,160]{2,1,0:T(8,128)} %constant.9.clone.ay_ref) | copy-start | bytes 122884

commit v5 on v4

--- a/solution.py
+++ b/solution.py
@@ -78,7 +78,7 @@
 
 
 def sum_block(pn, c, p, d, v_ref, az_ref, ay_ref, acc):
-    xt = 256
+    xt = 512
     wz = az_ref[p, c][: pn.nic]
     wy = ay_ref[d]
     w = (wz[:, None, :] * wy[None, :, :]).reshape(pn.nic * 8, pn.kk)

time: 80.9 us -> 75.9 us (0.938)
  Pallas kernels: 74.3 us -> 69.3 us
    pallas_call x1, Pallas kernels: 38.7 us -> 33.7 us  [local_sums(): pl.pallas_call(functools.partial(local_kernel, pn), grid=(pn.nch,), in_sp...]
where the time goes in v5:
time: 75.9 us; the launch traced here: 75.6 us
  Pallas kernels  69.3 us (91%)
  local copies, waits for them, and re-layouts  5.67 us (7%)
    pallas_call x1, Pallas kernels, exchange(): pl.pallas_call(functools.partial(exchange_kernel, pn), in_specs=[vmem], o...  35.6 us
    pallas_call x1, Pallas kernels, local_sums(): pl.pallas_call(functools.partial(local_kernel, pn), grid=(pn.nch,), in_sp...  33.7 us
    unnamed x10, local copies, waits for them, and re-layouts  5.67 us

profile of v5, /device:TPU:0, one launch (start us, length us, event | category | flops | bytes accessed | tf_op | source)
XLA Modules:
  0.0 75.6 jit_solution(4191337198173041775)
XLA Ops:
  0.6 0.0 copy-start
  0.6 1.2 %copy-done = bf16[2048,256]{1,0:T(8,128)(2,1)S(1)} copy-done((bf16[2048,256]{1,0:T(8,128)(2,1)S(1)}, bf16[2048,256]{1,0:T(8,128)(2,1)}, u32[]{:S(2)}) %copy-start) | copy-done | bytes 1048600
  1.9 0.0 copy-start.1
  1.9 1.2 %copy-done.1 = bf16[2048,256]{1,0:T(8,128)(2,1)S(1)} copy-done((bf16[2048,256]{1,0:T(8,128)(2,1)S(1)}, bf16[2048,256]{1,0:T(8,128)(2,1)}, u32[]{:S(2)}) %copy-start.1) | copy-done | bytes 1048600
  3.1 0.0 copy-start.2
  3.1 1.0 %copy-done.2 = f32[4,9,8,160]{3,2,1,0:T(8,128)S(1)} copy-done((f32[4,9,8,160]{3,2,1,0:T(8,128)S(1)}, f32[4,9,8,160]{3,2,1,0:T(8,128)}, u32[]{:S(2)}) %copy-start.2) | copy-done | bytes 184344
  4.0 0.0 copy-start.3
  4.0 0.8 %copy-done.3 = f32[8,8,160]{2,1,0:T(8,128)S(1)} copy-done((f32[8,8,160]{2,1,0:T(8,128)S(1)}, f32[8,8,160]{2,1,0:T(8,128)}, u32[]{:S(2)}) %copy-start.3) | copy-done | bytes 40984
  4.9 33.7 %shard_map.68.in_ref = f32[8,4,9,8,128]{4,3,2,1,0:T(8,128)S(1)} custom-call(f32[3,20,72,2048]{3,2,1,0:T(8,128)} %bitcast.1, f32[4,9,8,160]{3,2,1,0:T(8,128)S(1)} %copy-done.2, f32[8,8,160]{2,1,0:T(8,128)S(1)} %copy-done.3, bf16[2048,256]{1,0:T(8,128)(2,1)S(1)} %copy-done.1, bf16[2048,256]{1,0:T(8,128)(2,1)S(1)} %copy-done), custom_call_target="tpu_custom_call" | custom-call | tf_op jit(solution)/shard_map/pallas_call | solution.py:152
  38.6 35.6 %shard_map.69 = (f32[3,32,4,32]{3,2,1,0:T(4,128)S(1)}, f32[6,32,4,32]{3,2,1,0:T(4,128)S(1)}) custom-call(f32[8,4,9,8,128]{4,3,2,1,0:T(8,128)S(1)} %shard_map.68.in_ref), custom_call_target="tpu_custom_call" | custom-call | tf_op jit(solution)/shard_map/pallas_call | solution.py:230
  74.2 0.7 copy.9
  74.9 0.7 copy.10
Async XLA Ops:
  0.6 1.2 %copy-start = (bf16[2048,256]{1,0:T(8,128)(2,1)S(1)}, bf16[2048,256]{1,0:T(8,128)(2,1)}, u32[]{:S(2)}) copy-start(bf16[2048,256]{1,0:T(8,128)(2,1)} %constant.11.clone.wl_ref) | copy-start | bytes 3145732
  1.9 1.2 %copy-start.1 = (bf16[2048,256]{1,0:T(8,128)(2,1)S(1)}, bf16[2048,256]{1,0:T(8,128)(2,1)}, u32[]{:S(2)}) copy-start(bf16[2048,256]{1,0:T(8,128)(2,1)} %constant.10.clone.wh_ref) | copy-start | bytes 3145732
  3.1 1.0 %copy-start.2 = (f32[4,9,8,160]{3,2,1,0:T(8,128)S(1)}, f32[4,9,8,160]{3,2,1,0:T(8,128)}, u32[]{:S(2)}) copy-start(f32[4,9,8,160]{3,2,1,0:T(8,128)} %constant.8.clone.az_ref) | copy-start | bytes 552964
  4.0 0.8 %copy-start.3 = (f32[8,8,160]{2,1,0:T(8,128)S(1)}, f32[8,8,160]{2,1,0:T(8,128)}, u32[]{:S(2)}) copy-start(f32[8,8,160]{2,1,0:T(8,128)} %constant.9.clone.ay_ref) | copy-start | bytes 122884
